TPU v7x, 32 devices: a whole 2x2x4 slice. The times are simulated.
32 devices in a mesh: ax: 4 (over x, core), az: 8 (over z, y).
Axes of the slice: x: 2, y: 2, z: 4, core: 2. Of those that a mesh axis runs over, the one named last changes fastest.
Arguments:
- enthalpy: float32 [16, 1024, 256], P('ax', 'az'), may hold values from -2 to 2.5
- melting_status: int32 [16, 1024, 256], P('ax', 'az'), may hold values from 0 to 2
- plastic_flags: int32 [16, 1024, 256], P('ax', 'az'), may hold values 0 or 1
- displacement: float32 [2, 16, 1024, 256], P(None, 'ax', 'az'), may hold values from -3 to 3
Outputs:
- final_enthalpy: float32 [16, 1024, 256], P('ax', 'az')
- final_displacement: float32 [2, 16, 1024, 256], P(None, 'ax', 'az')
All inputs are finite; a program needn't handle non-finite values. No bound on the sum of `plastic_flags` on one device may be relied on, other than what follows from the above.
Results may differ from a plain program's by a relative error of at most 0.0003.
Values sent between devices are 32-bit elements; how exact they have to be, the bound alone decides.
A program may use at most 64 MiB of HBM per device.

v0:
```python
import jax
import jax.numpy as jnp
from jax import lax
from jax.sharding import PartitionSpec as P

HEAT_SWEEPS = 3
MECH_SWEEPS = 2


def with_halo(block, sides, width, periodic):
    for axis, dim in sides:
        count = lax.axis_size(axis)
        forward = [(i, i + 1) for i in range(count - 1)]
        if periodic:
            forward.append((count - 1, 0))
        backward = [(target, source) for source, target in forward]
        low = lax.ppermute(
            lax.slice_in_dim(block, block.shape[dim] - width, None, axis=dim), axis, forward
        )
        high = lax.ppermute(lax.slice_in_dim(block, 0, width, axis=dim), axis, backward)
        block = jnp.concatenate([low, block, high], axis=dim)
    return block


def phase_slope(melting_status):
    return jnp.where(melting_status == 0, 1.0, jnp.where(melting_status == 1, 0.08, 0.5))


def phase_offset(melting_status):
    return jnp.where(melting_status == 0, -1.0, jnp.where(melting_status == 1, -0.02, 0.0))


def voxel_kelvin(specific_energy_value, melting_status):
    return phase_slope(melting_status) * specific_energy_value + phase_offset(melting_status)


def conduct(stored_energy_array):
    return 1.0 + 0.6 * jax.nn.sigmoid(-4.0 * stored_energy_array)


def stiffness(stored_energy_array):
    return 1.0 + 3.0 * jax.nn.sigmoid(-3.0 * stored_energy_array)


def radial_heat(stored_energy_array):
    inner = jnp.full_like(stored_energy_array[..., :1], -2.0)
    radial_low = jnp.concatenate([inner, stored_energy_array[..., :-1]], axis=3)
    radial_high = jnp.concatenate(
        [stored_energy_array[..., 1:], stored_energy_array[..., -1:]], axis=3
    )
    return (radial_low, radial_high)


def heat_neighbours(stored_energy_array):
    planes = with_halo(stored_energy_array, (("ax", 1),), 1, False)
    cycle_pad = with_halo(stored_energy_array, (("az", 2),), 1, True)
    radial_low, radial_high = radial_heat(stored_energy_array)
    return [
        planes[:, :-2],
        planes[:, 2:],
        radial_low,
        radial_high,
        cycle_pad[:, :, :-2],
        cycle_pad[:, :, 2:],
    ]


def heat_flux(stored_energy_array, nearby):
    local_heat_conductance = conduct(stored_energy_array)
    return sum(
        (
            0.5 * (local_heat_conductance + conduct(near)) * (near - stored_energy_array)
            for near in nearby
        )
    )


def strip_neighbours(field, is_temp):
    planes = with_halo(field, (("ax", 1),), 1, False)
    cycle_pad = with_halo(field, (("az", 2),), 1, True)
    if is_temp:
        low_edge = field[..., :1]
        high_edge = field[..., -1:]
    else:
        low_edge = jnp.zeros_like(field[..., :1])
        high_edge = jnp.zeros_like(field[..., :1])
    radial_low = jnp.concatenate([low_edge, field[..., :-1]], axis=3)
    radial_high = jnp.concatenate([field[..., 1:], high_edge], axis=3)
    return [
        planes[:, :-2],
        planes[:, 2:],
        radial_low,
        radial_high,
        cycle_pad[:, :, :-2],
        cycle_pad[:, :, 2:],
    ]


def mechanics(stored_energy_array, creep_rate, disp_field):
    temp_near = strip_neighbours(stored_energy_array, True)
    modulus = stiffness(stored_energy_array)
    face_coef = [0.5 * (modulus + stiffness(near)) for near in temp_near]
    diagonal_total = 0.5 + sum(face_coef)
    body_force = jnp.concatenate(
        [
            0.5 * modulus * 0.5 * (temp_near[3] - temp_near[2]),
            0.5 * modulus * 0.5 * (temp_near[5] - temp_near[4]),
        ],
        axis=0,
    )
    yield_stress = 0.3 + 0.5 * jax.nn.sigmoid(-3.0 * stored_energy_array)
    for sweep_index in range(MECH_SWEEPS):
        disp_near = strip_neighbours(disp_field, False)
        strain = jnp.concatenate(
            [
                0.5 * (disp_near[3][0:1] - disp_near[2][0:1]),
                0.5 * (disp_near[5][1:2] - disp_near[4][1:2]),
            ],
            axis=0,
        )
        magnitude = jnp.sqrt(jnp.sum(strain * strain, axis=0, keepdims=True))
        overstress = jnp.maximum(modulus * magnitude - yield_stress, 0.0)
        plastic = creep_rate * overstress / (1.0 + creep_rate * modulus)
        correction = modulus * plastic * strain / jnp.maximum(magnitude, 0.1)
        adjacent_accumulated = sum((coef * near for coef, near in zip(face_coef, disp_near)))
        disp_field = (body_force + adjacent_accumulated - correction) / diagonal_total
    return disp_field


def on_device(enthalpy, melting_status, plastic_flags, displacement):
    freeze_status_spread = melting_status[None]
    specific_energy_value = enthalpy[None]
    for sweep_index in range(HEAT_SWEEPS):
        stored_energy_array = voxel_kelvin(specific_energy_value, freeze_status_spread)
        specific_energy_value = specific_energy_value + 0.08 * heat_flux(
            stored_energy_array, heat_neighbours(stored_energy_array)
        )
    stored_energy_array = voxel_kelvin(specific_energy_value, freeze_status_spread)
    creep_rate = (
        plastic_flags[None].astype(jnp.float32)
        * 0.6
        * jnp.exp(8.0 / 12.0 - 8.0 / (stored_energy_array + 12.0))
    )
    disp_out = mechanics(stored_energy_array, creep_rate, displacement)
    return (specific_energy_value[0], disp_out)


def solution(mesh):
    in_specs = (
        P("ax", "az", None),
        P("ax", "az", None),
        P("ax", "az", None),
        P(None, "ax", "az", None),
    )
    out_specs = (P("ax", "az", None), P(None, "ax", "az", None))
    return jax.shard_map(
        on_device, mesh=mesh, in_specs=in_specs, out_specs=out_specs, check_vma=False
    )
```

profile of v0, /device:TPU:1, one launch (start us, length us, event | category | flops | bytes accessed | tf_op | source)
XLA Modules:
  0.0 102.4 jit_solution(12472389135181380685)
XLA Ops:
  0.6 1.5 %fusion.170 = (f32[1,4,128,256]{3,2,1,0:T(8,128)S(1)}, pred[4,128,256]{2,1,0:T(8,128)(4,1)S(1)}, pred[4,128,256]{2,1,0:T(8,128)(4,1)S(1)}) fusion(f32[4,128,256]{2,1,0:T(8,128)} %param.4, s32[4,128,256]{2,1,0:T(8,128)} %param.5), kind=kLoop, calls=%fused_computation.246 | loop fusion | flops 1048576 | bytes 1835008 | tf_op jit(solution)/shard_map/add | solution.py:34
  2.2 0.7 fusion.196
  2.9 4.5 %collective-permute-start = (f32[1,1,128,256]{3,2,1,0:T(8,128)}, f32[1,1,128,256]{3,2,1,0:T(8,128)S(1)}, u32[]{:S(2)}, u32[]{:S(2)}) collective-permute-start(f32[1,1,128,256]{3,2,1,0:T(8,128)} %get-tuple-element.56), channel_id=1, source_target_pairs={{0,8},{8,16},{16,24},{1,9},{9,17},{17,25},{2,10},{10,18},{18,26},{... | collective-permute-start | bytes 393224 | tf_op jit(solution)/shard_map/ppermute | solution.py:17
  7.4 1.9 %collective-permute-start.1 = (f32[1,1,128,256]{3,2,1,0:T(8,128)}, f32[1,1,128,256]{3,2,1,0:T(8,128)}, u32[]{:S(2)}, u32[]{:S(2)}) collective-permute-start(f32[1,1,128,256]{3,2,1,0:T(8,128)} %get-tuple-element.57), channel_id=1, source_target_pairs={{8,0},{16,8},{24,16},{9,1},{17,9},{25,17},{10,2},{18,10},{26,18},{... | collective-permute-start | bytes 393224 | tf_op jit(solution)/shard_map/ppermute | solution.py:20
  9.3 0.6 fusion.198
  9.9 1.2 %collective-permute-start.2 = (f32[1,4,1,256]{3,2,1,0:T(1,128)}, f32[1,4,1,256]{3,2,1,0:T(1,128)}, u32[]{:S(2)}, u32[]{:S(2)}) collective-permute-start(f32[1,4,1,256]{3,2,1,0:T(1,128)} %get-tuple-element.60), channel_id=1, source_target_pairs={{0,1},{1,2},{2,3},{3,4},{4,5},{5,6},{6,7},{7,0},{8,9},{9,10},{10,1... | collective-permute-start | bytes 12296 | tf_op jit(solution)/shard_map/ppermute | solution.py:17
  11.2 3.1 %collective-permute-start.19 = (f32[2,4,1,256]{3,2,1,0:T(1,128)S(1)}, f32[2,4,1,256]{3,2,1,0:T(1,128)}, u32[]{:S(2)}, u32[]{:S(2)}) collective-permute-start(f32[2,4,1,256]{3,2,1,0:T(1,128)S(1)} %get-tuple-element.25), channel_id=1, source_target_pairs={{1,0},{2,1},{3,2},{4,3},{5,4},{6,5},{7,6},{0,7},{9,8},{10,9},{11,1... | collective-permute-start | bytes 24584 | tf_op jit(solution)/shard_map/ppermute | solution.py:20
  14.3 1.1 %fusion.197 = (f32[1,4,128,255]{3,2,1,0:T(8,128)}, f32[4,128,255]{2,1,0:T(8,128)}) fusion(f32[1,4,128,256]{3,2,1,0:T(8,128)S(1)} %get-tuple-element.9), kind=kLoop, calls=%fused_computation.274 | loop fusion | bytes 2088960 | tf_op jit(solution)/shard_map/slice | solution.py:47
  15.4 0.9 slice_bitcast_fusion.1
  16.3 0.3 fusion.184
  16.6 1.1 %constant_dynamic-update-slice_fusion = f32[2,4,129,256]{3,2,1,0:T(8,128)} fusion(f32[2,4,128,256]{3,2,1,0:T(8,128)S(1)} %copy-done), kind=kLoop, calls=%fused_computation.250 | loop fusion | bytes 2097152
  17.8 0.8 fusion.183
  18.6 0.2 fusion.27
  18.9 4.2 %collective-permute-start.3 = (f32[1,4,1,256]{3,2,1,0:T(1,128)}, f32[1,4,1,256]{3,2,1,0:T(1,128)}, u32[]{:S(2)}, u32[]{:S(2)}) collective-permute-start(f32[1,4,1,256]{3,2,1,0:T(1,128)} %get-tuple-element.61), channel_id=1, source_target_pairs={{1,0},{2,1},{3,2},{4,3},{5,4},{6,5},{7,6},{0,7},{9,8},{10,9},{11,1... | collective-permute-start | bytes 12296 | tf_op jit(solution)/shard_map/ppermute | solution.py:20
  23.1 1.5 %dynamic-update-slice.1 = f32[2,4,129,256]{3,2,1,0:T(8,128)} dynamic-update-slice(f32[2,4,129,256]{3,2,1,0:T(8,128)} %constant_dynamic-update-slice_fusion, f32[2,4,1,256]{3,2,1,0:T(1,128)} %collective-permute-done.19, s32[]{} %constant.63, s32[]{} %constant.63, s32[]{} %constant.64, s32[]{} %constant.63) | dynamic-update-slice | bytes 16388 | tf_op jit(solution)/shard_map/concatenate | solution.py:21
  24.6 4.6 %collective-permute-start.15 = (f32[2,1,128,256]{3,2,1,0:T(8,128)}, f32[2,1,128,256]{3,2,1,0:T(8,128)S(1)}, u32[]{:S(2)}, u32[]{:S(2)}) collective-permute-start(f32[2,1,128,256]{3,2,1,0:T(8,128)} %get-tuple-element.21), channel_id=1, source_target_pairs={{0,8},{8,16},{16,24},{1,9},{9,17},{17,25},{2,10},{10,18},{18,26},{... | collective-permute-start | bytes 786440 | tf_op jit(solution)/shard_map/ppermute | solution.py:17
  29.2 1.2 %fusion.33 = f32[1,4,128,256]{3,2,1,0:T(8,128)S(1)} fusion(f32[2,4,128,256]{3,2,1,0:T(8,128)S(1)} %copy-done, f32[2,4,1,256]{3,2,1,0:T(1,128)S(1)} %collective-permute-done.18, f32[2,4,129,256]{3,2,1,0:T(8,128)} %dynamic-update-slice.1), kind=kLoop, calls=%fused_computation.56 | loop fusion | flops 393216 | bytes 2105344 | tf_op jit(solution)/shard_map/mul | solution.py:117
  30.4 0.1 multiply_reduce_fusion.1
  30.5 0.1 sqrt_maximum_fusion.1
  30.7 0.7 copy-done.4
  31.4 0.2 copy-done.5
  31.6 0.2 copy-done.6
  31.7 0.1 copy-done.8
  31.8 2.8 %bitcast_add_fusion.2 = (f32[1,4,128,256]{3,2,1,0:T(8,128)S(1)}, f32[1,4,128,256]{3,2,1,0:T(8,128)S(1)}) fusion(pred[4,128,256]{2,1,0:T(8,128)(4,1)S(1)} %get-tuple-element.11, pred[4,128,256]{2,1,0:T(8,128)(4,1)S(1)} %get-tuple-element.10, f32[1,4,128,256]{3,2,1,0:T(8,128)S(1)} %get-tuple-element.9, f32[1,4,1,256]{3,2,1,0:T(1,128)} %collective-permute-done.3, ...), kind=kLoop, calls=%fused_computation.213 | loop fusion | flops 11272192 | bytes 3676160 | tf_op jit(solution)/shard_map/add | solution.py:34
  34.6 1.9 %collective-permute-start.4 = (f32[1,1,128,256]{3,2,1,0:T(8,128)S(1)}, f32[1,1,128,256]{3,2,1,0:T(8,128)S(1)}, u32[]{:S(2)}, u32[]{:S(2)}) collective-permute-start(f32[1,1,128,256]{3,2,1,0:T(8,128)S(1)} %get-tuple-element.50), channel_id=1, source_target_pairs={{0,8},{8,16},{16,24},{1,9},{9,17},{17,25},{2,10},{10,18},{18,26},{... | collective-permute-start | bytes 393224 | tf_op jit(solution)/shard_map/ppermute | solution.py:17
  36.6 2.4 %collective-permute-start.5 = (f32[1,1,128,256]{3,2,1,0:T(8,128)S(1)}, f32[1,1,128,256]{3,2,1,0:T(8,128)S(1)}, u32[]{:S(2)}, u32[]{:S(2)}) collective-permute-start(f32[1,1,128,256]{3,2,1,0:T(8,128)S(1)} %get-tuple-element.51), channel_id=1, source_target_pairs={{8,0},{16,8},{24,16},{9,1},{17,9},{25,17},{10,2},{18,10},{26,18},{... | collective-permute-start | bytes 393224 | tf_op jit(solution)/shard_map/ppermute | solution.py:20
  39.0 0.1 collective-permute-start.6
  39.0 4.1 %collective-permute-start.7 = (f32[1,4,1,256]{3,2,1,0:T(1,128)S(1)}, f32[1,4,1,256]{3,2,1,0:T(1,128)S(1)}, u32[]{:S(2)}, u32[]{:S(2)}) collective-permute-start(f32[1,4,1,256]{3,2,1,0:T(1,128)S(1)} %get-tuple-element.55), channel_id=1, source_target_pairs={{1,0},{2,1},{3,2},{4,3},{5,4},{6,5},{7,6},{0,7},{9,8},{10,9},{11,1... | collective-permute-start | bytes 12296 | tf_op jit(solution)/shard_map/ppermute | solution.py:20
  43.2 0.2 fusion.194
  43.4 0.1 slice.331
  43.5 0.8 collective-permute-done.6
  44.3 1.9 %bitcast_add_fusion.1 = (f32[1,4,128,256]{3,2,1,0:T(8,128)S(1)}, f32[1,4,128,256]{3,2,1,0:T(8,128)S(1)}) fusion(pred[4,128,256]{2,1,0:T(8,128)(4,1)S(1)} %get-tuple-element.11, pred[4,128,256]{2,1,0:T(8,128)(4,1)S(1)} %get-tuple-element.10, f32[1,4,128,256]{3,2,1,0:T(8,128)S(1)} %get-tuple-element.8, f32[1,4,128,256]{3,2,1,0:T(8,128)S(1)} %get-tuple-element.7, ...), kind=kLoop, calls=%fused_computation.212 | loop fusion | flops 11010048 | bytes 3676160 | tf_op jit(solution)/shard_map/add | solution.py:34
  46.3 4.2 %collective-permute-start.8 = (f32[1,1,128,256]{3,2,1,0:T(8,128)S(1)}, f32[1,1,128,256]{3,2,1,0:T(8,128)S(1)}, u32[]{:S(2)}, u32[]{:S(2)}) collective-permute-start(f32[1,1,128,256]{3,2,1,0:T(8,128)S(1)} %get-tuple-element.44), channel_id=1, source_target_pairs={{0,8},{8,16},{16,24},{1,9},{9,17},{17,25},{2,10},{10,18},{18,26},{... | collective-permute-start | bytes 393224 | tf_op jit(solution)/shard_map/ppermute | solution.py:17
  50.5 1.9 %collective-permute-start.9 = (f32[1,1,128,256]{3,2,1,0:T(8,128)S(1)}, f32[1,1,128,256]{3,2,1,0:T(8,128)S(1)}, u32[]{:S(2)}, u32[]{:S(2)}) collective-permute-start(f32[1,1,128,256]{3,2,1,0:T(8,128)S(1)} %get-tuple-element.45), channel_id=1, source_target_pairs={{8,0},{16,8},{24,16},{9,1},{17,9},{25,17},{10,2},{18,10},{26,18},{... | collective-permute-start | bytes 393224 | tf_op jit(solution)/shard_map/ppermute | solution.py:20
  52.4 0.1 collective-permute-start.10
  52.5 4.5 %collective-permute-start.11 = (f32[1,4,1,256]{3,2,1,0:T(1,128)S(1)}, f32[1,4,1,256]{3,2,1,0:T(1,128)S(1)}, u32[]{:S(2)}, u32[]{:S(2)}) collective-permute-start(f32[1,4,1,256]{3,2,1,0:T(1,128)S(1)} %get-tuple-element.49), channel_id=1, source_target_pairs={{1,0},{2,1},{3,2},{4,3},{5,4},{6,5},{7,6},{0,7},{9,8},{10,9},{11,1... | collective-permute-start | bytes 12296 | tf_op jit(solution)/shard_map/ppermute | solution.py:20
  57.0 0.2 fusion.191
  57.2 0.1 slice.338
  57.3 0.6 collective-permute-done.10
  57.9 3.2 %fusion.162 = (f32[4,128,256]{2,1,0:T(8,128)S(1)}, f32[1,4,128,256]{3,2,1,0:T(8,128)S(1)}, f32[1,4,128,256]{3,2,1,0:T(8,128)}) fusion(f32[4,128,256]{2,1,0:T(8,128)S(1)} %multiply_reduce_fusion.1, s32[4,128,256]{2,1,0:T(8,128)S(1)} %copy-done.7, pred[4,128,256]{2,1,0:T(8,128)(4,1)S(1)} %get-tuple-element.11, pred[4,128,256]{2,1,0:T(8,128)(4,1)S(1)} %get-tuple-element.10, ...), kind=kLoop, calls=%fused_computation.209 | loop fusion | flops 13893632 | bytes 5249024 | tf_op jit(solution)/shard_map/mul | solution.py:124
  61.1 0.2 fusion.187
  61.4 4.7 %collective-permute-start.14 = (f32[1,1,128,256]{3,2,1,0:T(8,128)S(1)}, f32[1,1,128,256]{3,2,1,0:T(8,128)S(1)}, u32[]{:S(2)}, u32[]{:S(2)}) collective-permute-start(f32[1,1,128,256]{3,2,1,0:T(8,128)S(1)} %get-tuple-element.37), channel_id=1, source_target_pairs={{0,8},{8,16},{16,24},{1,9},{9,17},{17,25},{2,10},{10,18},{18,26},{... | collective-permute-start | bytes 393224 | tf_op jit(solution)/shard_map/ppermute | solution.py:17
  66.1 1.9 %collective-permute-start.16 = (f32[1,1,128,256]{3,2,1,0:T(8,128)S(1)}, f32[1,1,128,256]{3,2,1,0:T(8,128)S(1)}, u32[]{:S(2)}, u32[]{:S(2)}) collective-permute-start(f32[1,1,128,256]{3,2,1,0:T(8,128)S(1)} %get-tuple-element.36), channel_id=1, source_target_pairs={{8,0},{16,8},{24,16},{9,1},{17,9},{25,17},{10,2},{18,10},{26,18},{... | collective-permute-start | bytes 393224 | tf_op jit(solution)/shard_map/ppermute | solution.py:20
  68.0 4.5 %collective-permute-start.12 = (f32[1,4,1,256]{3,2,1,0:T(1,128)S(1)}, f32[1,4,1,256]{3,2,1,0:T(1,128)S(1)}, u32[]{:S(2)}, u32[]{:S(2)}) collective-permute-start(f32[1,4,1,256]{3,2,1,0:T(1,128)S(1)} %get-tuple-element.43), channel_id=1, source_target_pairs={{1,0},{2,1},{3,2},{4,3},{5,4},{6,5},{7,6},{0,7},{9,8},{10,9},{11,1... | collective-permute-start | bytes 12296 | tf_op jit(solution)/shard_map/ppermute | solution.py:20
  72.5 0.1 fusion.188
  72.7 0.6 collective-permute-done.12
  73.3 1.9 %collective-permute-start.17 = (f32[2,1,128,256]{3,2,1,0:T(8,128)S(1)}, f32[2,1,128,256]{3,2,1,0:T(8,128)S(1)}, u32[]{:S(2)}, u32[]{:S(2)}) collective-permute-start(f32[2,1,128,256]{3,2,1,0:T(8,128)S(1)} %copy-done.9), channel_id=1, source_target_pairs={{8,0},{16,8},{24,16},{9,1},{17,9},{25,17},{10,2},{18,10},{26,18},{... | collective-permute-start | bytes 786440 | tf_op jit(solution)/shard_map/ppermute | solution.py:20
  75.2 2.5 %collective-permute-done.13 = f32[1,4,1,256]{3,2,1,0:T(1,128)S(1)} collective-permute-done((f32[1,4,1,256]{3,2,1,0:T(1,128)S(1)}, f32[1,4,1,256]{3,2,1,0:T(1,128)S(1)}, u32[]{:S(2)}, u32[]{:S(2)}) %collective-permute-start.13) | collective-permute-done | bytes 4128 | tf_op jit(solution)/shard_map/ppermute | solution.py:17
  77.7 1.2 %add_bitcast_fusion = (f32[4,128,256]{2,1,0:T(8,128)S(1)}, f32[1,4,128,256]{3,2,1,0:T(8,128)S(1)}, f32[4,128,256]{2,1,0:T(8,128)S(1)}) fusion(f32[1,4,128,256]{3,2,1,0:T(8,128)S(1)} %get-tuple-element.3, f32[1,4,1,256]{3,2,1,0:T(1,128)S(1)} %collective-permute-done.13, f32[1,4,1,256]{3,2,1,0:T(1,128)S(1)} %collective-permute-done.12, ...), kind=kLoop, calls=%fused_computation.228 | loop fusion | flops 9043968 | bytes 3416064 | tf_op jit(solution)/shard_map/div | solution.py:126
  78.9 1.0 fusion.173
  79.9 1.9 %collective-permute-done.17 = f32[2,1,128,256]{3,2,1,0:T(8,128)S(1)} collective-permute-done((f32[2,1,128,256]{3,2,1,0:T(8,128)S(1)}, f32[2,1,128,256]{3,2,1,0:T(8,128)S(1)}, u32[]{:S(2)}, u32[]{:S(2)}) %collective-permute-start.17) | collective-permute-done | bytes 262176 | tf_op jit(solution)/shard_map/ppermute | solution.py:20
  81.8 1.6 %fusion.15 = f32[2,4,128,256]{3,2,1,0:T(8,128)S(1)} fusion(f32[2,4,1,256]{3,2,1,0:T(1,128)S(1)} %collective-permute-done.18, f32[2,4,128,256]{3,2,1,0:T(8,128)S(1)} %copy-done, f32[2,4,129,256]{3,2,1,0:T(8,128)S(1)} %copy-done.3, f32[2,1,128,256]{3,2,1,0:T(8,128)S(1)} %collective-permute-done.17, f32[2,1,128,256]{3,2,1,0:T(8,128)S(1)} %collective-permute-done.15, ...), kind=kLoop, calls=%fused_computation.21 | loop fusion | flops 5505024 | bytes 12582912 | tf_op jit(solution)/shard_map/div | solution.py:126
  83.4 0.4 fusion.180
  83.9 4.7 %collective-permute-start.23 = (f32[2,4,1,256]{3,2,1,0:T(1,128)S(1)}, f32[2,4,1,256]{3,2,1,0:T(1,128)S(1)}, u32[]{:S(2)}, u32[]{:S(2)}) collective-permute-start(f32[2,4,1,256]{3,2,1,0:T(1,128)S(1)} %get-tuple-element.20), channel_id=1, source_target_pairs={{1,0},{2,1},{3,2},{4,3},{5,4},{6,5},{7,6},{0,7},{9,8},{10,9},{11,1... | collective-permute-start | bytes 24584 | tf_op jit(solution)/shard_map/ppermute | solution.py:20
  88.6 3.7 %collective-permute-start.20 = (f32[2,1,128,256]{3,2,1,0:T(8,128)S(1)}, f32[2,1,128,256]{3,2,1,0:T(8,128)S(1)}, u32[]{:S(2)}, u32[]{:S(2)}) collective-permute-start(f32[2,1,128,256]{3,2,1,0:T(8,128)S(1)} %get-tuple-element.17), channel_id=1, source_target_pairs={{0,8},{8,16},{16,24},{1,9},{9,17},{17,25},{2,10},{10,18},{18,26},{... | collective-permute-start | bytes 786440 | tf_op jit(solution)/shard_map/ppermute | solution.py:17
  92.3 1.9 %collective-permute-start.21 = (f32[2,1,128,256]{3,2,1,0:T(8,128)S(1)}, f32[2,1,128,256]{3,2,1,0:T(8,128)S(1)}, u32[]{:S(2)}, u32[]{:S(2)}) collective-permute-start(f32[2,1,128,256]{3,2,1,0:T(8,128)S(1)} %get-tuple-element.18), channel_id=1, source_target_pairs={{8,0},{16,8},{24,16},{9,1},{17,9},{25,17},{10,2},{18,10},{26,18},{... | collective-permute-start | bytes 786440 | tf_op jit(solution)/shard_map/ppermute | solution.py:20
  94.2 0.2 fusion.29
  94.5 0.1 fusion.31
  94.6 0.1 multiply_reduce_fusion
  94.7 0.6 fusion.156
  95.3 0.1 sqrt_maximum_fusion
  95.4 0.2 collective-permute-done.20
  95.6 4.4 %collective-permute-done.21 = f32[2,1,128,256]{3,2,1,0:T(8,128)S(1)} collective-permute-done((f32[2,1,128,256]{3,2,1,0:T(8,128)S(1)}, f32[2,1,128,256]{3,2,1,0:T(8,128)S(1)}, u32[]{:S(2)}, u32[]{:S(2)}) %collective-permute-start.21) | collective-permute-done | bytes 262176 | tf_op jit(solution)/shard_map/ppermute | solution.py:20
  100.0 2.4 %fusion.5 = f32[2,4,128,256]{3,2,1,0:T(8,128)} fusion(f32[2,4,128,256]{3,2,1,0:T(8,128)S(1)} %fusion.15, f32[2,4,1,256]{3,2,1,0:T(1,128)S(1)} %collective-permute-done.23, f32[2,4,1,256]{3,2,1,0:T(1,128)S(1)} %collective-permute-done.22, f32[2,1,128,256]{3,2,1,0:T(8,128)S(1)} %collective-permute-done.21, f32[2,1,128,256]{3,2,1,0:T(8,128)S(1)} %collective-permute-done.20, ...), kind=kLoop, calls=%fused_computation.11 | loop fusion | flops 5767168 | bytes 11542528 | tf_op jit(solution)/shard_map/div | solution.py:126
  (45 shorter events, 0.3 us)
Async XLA Ops:
  0.6 10.6 %copy-start = (f32[2,4,128,256]{3,2,1,0:T(8,128)S(1)}, f32[2,4,128,256]{3,2,1,0:T(8,128)}, u32[]{:S(2)}) copy-start(f32[2,4,128,256]{3,2,1,0:T(8,128)} %param.7) | copy-start | bytes 3145732
  2.9 27.8 %collective-permute-start = (f32[1,1,128,256]{3,2,1,0:T(8,128)}, f32[1,1,128,256]{3,2,1,0:T(8,128)S(1)}, u32[]{:S(2)}, u32[]{:S(2)}) collective-permute-start(f32[1,1,128,256]{3,2,1,0:T(8,128)} %get-tuple-element.56), channel_id=1, source_target_pairs={{0,8},{8,16},{16,24},{1,9},{9,17},{17,25},{2,10},{10,18},{18,26},{... | collective-permute-start | bytes 393224 | tf_op jit(solution)/shard_map/ppermute | solution.py:17
  7.4 23.3 %collective-permute-start.1 = (f32[1,1,128,256]{3,2,1,0:T(8,128)}, f32[1,1,128,256]{3,2,1,0:T(8,128)}, u32[]{:S(2)}, u32[]{:S(2)}) collective-permute-start(f32[1,1,128,256]{3,2,1,0:T(8,128)} %get-tuple-element.57), channel_id=1, source_target_pairs={{8,0},{16,8},{24,16},{9,1},{17,9},{25,17},{10,2},{18,10},{26,18},{... | collective-permute-start | bytes 393224 | tf_op jit(solution)/shard_map/ppermute | solution.py:20
  9.9 20.7 %collective-permute-start.2 = (f32[1,4,1,256]{3,2,1,0:T(1,128)}, f32[1,4,1,256]{3,2,1,0:T(1,128)}, u32[]{:S(2)}, u32[]{:S(2)}) collective-permute-start(f32[1,4,1,256]{3,2,1,0:T(1,128)} %get-tuple-element.60), channel_id=1, source_target_pairs={{0,1},{1,2},{2,3},{3,4},{4,5},{5,6},{6,7},{7,0},{8,9},{9,10},{10,1... | collective-permute-start | bytes 12296 | tf_op jit(solution)/shard_map/ppermute | solution.py:17
  11.2 7.7 %collective-permute-start.19 = (f32[2,4,1,256]{3,2,1,0:T(1,128)S(1)}, f32[2,4,1,256]{3,2,1,0:T(1,128)}, u32[]{:S(2)}, u32[]{:S(2)}) collective-permute-start(f32[2,4,1,256]{3,2,1,0:T(1,128)S(1)} %get-tuple-element.25), channel_id=1, source_target_pairs={{1,0},{2,1},{3,2},{4,3},{5,4},{6,5},{7,6},{0,7},{9,8},{10,9},{11,1... | collective-permute-start | bytes 24584 | tf_op jit(solution)/shard_map/ppermute | solution.py:20
  14.3 10.3 %collective-permute-start.18 = (f32[2,4,1,256]{3,2,1,0:T(1,128)S(1)}, f32[2,4,1,256]{3,2,1,0:T(1,128)S(1)}, u32[]{:S(2)}, u32[]{:S(2)}) collective-permute-start(f32[2,4,1,256]{3,2,1,0:T(1,128)S(1)} %get-tuple-element.26), channel_id=1, source_target_pairs={{0,1},{1,2},{2,3},{3,4},{4,5},{5,6},{6,7},{7,0},{8,9},{9,10},{10,1... | collective-permute-start | bytes 24584 | tf_op jit(solution)/shard_map/ppermute | solution.py:17
  16.6 2.0 %copy-start.1 = (f32[2,4,128,255]{3,2,1,0:T(8,128)}, f32[2,4,128,255]{3,2,1,0:T(8,128)S(1)}, u32[]{:S(2)}) copy-start(f32[2,4,128,255]{3,2,1,0:T(8,128)S(1)} %get-tuple-element.24) | copy-start | bytes 3133444
  18.9 11.8 %collective-permute-start.3 = (f32[1,4,1,256]{3,2,1,0:T(1,128)}, f32[1,4,1,256]{3,2,1,0:T(1,128)}, u32[]{:S(2)}, u32[]{:S(2)}) collective-permute-start(f32[1,4,1,256]{3,2,1,0:T(1,128)} %get-tuple-element.61), channel_id=1, source_target_pairs={{1,0},{2,1},{3,2},{4,3},{5,4},{6,5},{7,6},{0,7},{9,8},{10,9},{11,1... | collective-permute-start | bytes 12296 | tf_op jit(solution)/shard_map/ppermute | solution.py:20
  24.6 55.3 %collective-permute-start.15 = (f32[2,1,128,256]{3,2,1,0:T(8,128)}, f32[2,1,128,256]{3,2,1,0:T(8,128)S(1)}, u32[]{:S(2)}, u32[]{:S(2)}) collective-permute-start(f32[2,1,128,256]{3,2,1,0:T(8,128)} %get-tuple-element.21), channel_id=1, source_target_pairs={{0,8},{8,16},{16,24},{1,9},{9,17},{17,25},{2,10},{10,18},{18,26},{... | collective-permute-start | bytes 786440 | tf_op jit(solution)/shard_map/ppermute | solution.py:17
  30.4 1.0 %copy-start.4 = (f32[4,128,256]{2,1,0:T(8,128)S(1)}, f32[4,128,256]{2,1,0:T(8,128)}, u32[]{:S(2)}) copy-start(f32[4,128,256]{2,1,0:T(8,128)} %param.4) | copy-start | bytes 1572868
  30.4 1.2 %copy-start.5 = (f32[1,4,128,255]{3,2,1,0:T(8,128)S(1)}, f32[1,4,128,255]{3,2,1,0:T(8,128)}, u32[]{:S(2)}) copy-start(f32[1,4,128,255]{3,2,1,0:T(8,128)} %get-tuple-element.58) | copy-start | bytes 1566724
  30.4 1.3 %copy-start.6 = (f32[4,128,255]{2,1,0:T(8,128)S(1)}, f32[4,128,255]{2,1,0:T(8,128)}, u32[]{:S(2)}) copy-start(f32[4,128,255]{2,1,0:T(8,128)} %get-tuple-element.59) | copy-start | bytes 1566724
  30.4 1.4 %copy-start.8 = (f32[4,128,1]{2,1,0:T(8,128)S(1)}, f32[4,128,1]{2,1,0:T(8,128)}, u32[]{:S(2)}) copy-start(f32[4,128,1]{2,1,0:T(8,128)} %slice_bitcast_fusion.1) | copy-start | bytes 6148
  34.6 9.7 %collective-permute-start.4 = (f32[1,1,128,256]{3,2,1,0:T(8,128)S(1)}, f32[1,1,128,256]{3,2,1,0:T(8,128)S(1)}, u32[]{:S(2)}, u32[]{:S(2)}) collective-permute-start(f32[1,1,128,256]{3,2,1,0:T(8,128)S(1)} %get-tuple-element.50), channel_id=1, source_target_pairs={{0,8},{8,16},{16,24},{1,9},{9,17},{17,25},{2,10},{10,18},{18,26},{... | collective-permute-start | bytes 393224 | tf_op jit(solution)/shard_map/ppermute | solution.py:17
  36.6 7.8 %collective-permute-start.5 = (f32[1,1,128,256]{3,2,1,0:T(8,128)S(1)}, f32[1,1,128,256]{3,2,1,0:T(8,128)S(1)}, u32[]{:S(2)}, u32[]{:S(2)}) collective-permute-start(f32[1,1,128,256]{3,2,1,0:T(8,128)S(1)} %get-tuple-element.51), channel_id=1, source_target_pairs={{8,0},{16,8},{24,16},{9,1},{17,9},{25,17},{10,2},{18,10},{26,18},{... | collective-permute-start | bytes 393224 | tf_op jit(solution)/shard_map/ppermute | solution.py:20
  39.0 5.3 %collective-permute-start.6 = (f32[1,4,1,256]{3,2,1,0:T(1,128)S(1)}, f32[1,4,1,256]{3,2,1,0:T(1,128)S(1)}, u32[]{:S(2)}, u32[]{:S(2)}) collective-permute-start(f32[1,4,1,256]{3,2,1,0:T(1,128)S(1)} %get-tuple-element.54), channel_id=1, source_target_pairs={{0,1},{1,2},{2,3},{3,4},{4,5},{5,6},{6,7},{7,0},{8,9},{9,10},{10,1... | collective-permute-start | bytes 12296 | tf_op jit(solution)/shard_map/ppermute | solution.py:17
  39.0 5.3 %collective-permute-start.7 = (f32[1,4,1,256]{3,2,1,0:T(1,128)S(1)}, f32[1,4,1,256]{3,2,1,0:T(1,128)S(1)}, u32[]{:S(2)}, u32[]{:S(2)}) collective-permute-start(f32[1,4,1,256]{3,2,1,0:T(1,128)S(1)} %get-tuple-element.55), channel_id=1, source_target_pairs={{1,0},{2,1},{3,2},{4,3},{5,4},{6,5},{7,6},{0,7},{9,8},{10,9},{11,1... | collective-permute-start | bytes 12296 | tf_op jit(solution)/shard_map/ppermute | solution.py:20
  46.3 11.6 %collective-permute-start.8 = (f32[1,1,128,256]{3,2,1,0:T(8,128)S(1)}, f32[1,1,128,256]{3,2,1,0:T(8,128)S(1)}, u32[]{:S(2)}, u32[]{:S(2)}) collective-permute-start(f32[1,1,128,256]{3,2,1,0:T(8,128)S(1)} %get-tuple-element.44), channel_id=1, source_target_pairs={{0,8},{8,16},{16,24},{1,9},{9,17},{17,25},{2,10},{10,18},{18,26},{... | collective-permute-start | bytes 393224 | tf_op jit(solution)/shard_map/ppermute | solution.py:17
  50.5 7.4 %collective-permute-start.9 = (f32[1,1,128,256]{3,2,1,0:T(8,128)S(1)}, f32[1,1,128,256]{3,2,1,0:T(8,128)S(1)}, u32[]{:S(2)}, u32[]{:S(2)}) collective-permute-start(f32[1,1,128,256]{3,2,1,0:T(8,128)S(1)} %get-tuple-element.45), channel_id=1, source_target_pairs={{8,0},{16,8},{24,16},{9,1},{17,9},{25,17},{10,2},{18,10},{26,18},{... | collective-permute-start | bytes 393224 | tf_op jit(solution)/shard_map/ppermute | solution.py:20
  52.4 5.5 %collective-permute-start.10 = (f32[1,4,1,256]{3,2,1,0:T(1,128)S(1)}, f32[1,4,1,256]{3,2,1,0:T(1,128)S(1)}, u32[]{:S(2)}, u32[]{:S(2)}) collective-permute-start(f32[1,4,1,256]{3,2,1,0:T(1,128)S(1)} %get-tuple-element.48), channel_id=1, source_target_pairs={{0,1},{1,2},{2,3},{3,4},{4,5},{5,6},{6,7},{7,0},{8,9},{9,10},{10,1... | collective-permute-start | bytes 12296 | tf_op jit(solution)/shard_map/ppermute | solution.py:17
  52.5 5.4 %copy-start.7 = (s32[4,128,256]{2,1,0:T(8,128)S(1)}, s32[4,128,256]{2,1,0:T(8,128)}, u32[]{:S(2)}) copy-start(s32[4,128,256]{2,1,0:T(8,128)} %param.6) | copy-start | bytes 1572868
  52.5 5.4 %collective-permute-start.11 = (f32[1,4,1,256]{3,2,1,0:T(1,128)S(1)}, f32[1,4,1,256]{3,2,1,0:T(1,128)S(1)}, u32[]{:S(2)}, u32[]{:S(2)}) collective-permute-start(f32[1,4,1,256]{3,2,1,0:T(1,128)S(1)} %get-tuple-element.49), channel_id=1, source_target_pairs={{1,0},{2,1},{3,2},{4,3},{5,4},{6,5},{7,6},{0,7},{9,8},{10,9},{11,1... | collective-permute-start | bytes 12296 | tf_op jit(solution)/shard_map/ppermute | solution.py:20
  61.4 11.9 %copy-start.9 = (f32[2,1,128,256]{3,2,1,0:T(8,128)S(1)}, f32[2,1,128,256]{3,2,1,0:T(8,128)}, u32[]{:S(2)}) copy-start(f32[2,1,128,256]{3,2,1,0:T(8,128)} %get-tuple-element.22) | copy-start | bytes 786436
  61.4 16.3 %collective-permute-start.14 = (f32[1,1,128,256]{3,2,1,0:T(8,128)S(1)}, f32[1,1,128,256]{3,2,1,0:T(8,128)S(1)}, u32[]{:S(2)}, u32[]{:S(2)}) collective-permute-start(f32[1,1,128,256]{3,2,1,0:T(8,128)S(1)} %get-tuple-element.37), channel_id=1, source_target_pairs={{0,8},{8,16},{16,24},{1,9},{9,17},{17,25},{2,10},{10,18},{18,26},{... | collective-permute-start | bytes 393224 | tf_op jit(solution)/shard_map/ppermute | solution.py:17
  66.1 11.6 %collective-permute-start.16 = (f32[1,1,128,256]{3,2,1,0:T(8,128)S(1)}, f32[1,1,128,256]{3,2,1,0:T(8,128)S(1)}, u32[]{:S(2)}, u32[]{:S(2)}) collective-permute-start(f32[1,1,128,256]{3,2,1,0:T(8,128)S(1)} %get-tuple-element.36), channel_id=1, source_target_pairs={{8,0},{16,8},{24,16},{9,1},{17,9},{25,17},{10,2},{18,10},{26,18},{... | collective-permute-start | bytes 393224 | tf_op jit(solution)/shard_map/ppermute | solution.py:20
  68.0 5.3 %collective-permute-start.12 = (f32[1,4,1,256]{3,2,1,0:T(1,128)S(1)}, f32[1,4,1,256]{3,2,1,0:T(1,128)S(1)}, u32[]{:S(2)}, u32[]{:S(2)}) collective-permute-start(f32[1,4,1,256]{3,2,1,0:T(1,128)S(1)} %get-tuple-element.43), channel_id=1, source_target_pairs={{1,0},{2,1},{3,2},{4,3},{5,4},{6,5},{7,6},{0,7},{9,8},{10,9},{11,1... | collective-permute-start | bytes 12296 | tf_op jit(solution)/shard_map/ppermute | solution.py:20
  72.5 5.2 %collective-permute-start.13 = (f32[1,4,1,256]{3,2,1,0:T(1,128)S(1)}, f32[1,4,1,256]{3,2,1,0:T(1,128)S(1)}, u32[]{:S(2)}, u32[]{:S(2)}) collective-permute-start(f32[1,4,1,256]{3,2,1,0:T(1,128)S(1)} %get-tuple-element.42), channel_id=1, source_target_pairs={{0,1},{1,2},{2,3},{3,4},{4,5},{5,6},{6,7},{7,0},{8,9},{9,10},{10,1... | collective-permute-start | bytes 12296 | tf_op jit(solution)/shard_map/ppermute | solution.py:17
  73.3 8.5 %collective-permute-start.17 = (f32[2,1,128,256]{3,2,1,0:T(8,128)S(1)}, f32[2,1,128,256]{3,2,1,0:T(8,128)S(1)}, u32[]{:S(2)}, u32[]{:S(2)}) collective-permute-start(f32[2,1,128,256]{3,2,1,0:T(8,128)S(1)} %copy-done.9), channel_id=1, source_target_pairs={{8,0},{16,8},{24,16},{9,1},{17,9},{25,17},{10,2},{18,10},{26,18},{... | collective-permute-start | bytes 786440 | tf_op jit(solution)/shard_map/ppermute | solution.py:20
  78.9 2.9 %copy-start.2 = (f32[2,4,128,255]{3,2,1,0:T(8,128)S(1)}, f32[2,4,128,255]{3,2,1,0:T(8,128)}, u32[]{:S(2)}) copy-start(f32[2,4,128,255]{3,2,1,0:T(8,128)} %copy-done.1) | copy-start | bytes 3133444
  78.9 2.9 %copy-start.3 = (f32[2,4,129,256]{3,2,1,0:T(8,128)S(1)}, f32[2,4,129,256]{3,2,1,0:T(8,128)}, u32[]{:S(2)}) copy-start(f32[2,4,129,256]{3,2,1,0:T(8,128)} %dynamic-update-slice.1) | copy-start | bytes 3170308
  83.8 10.6 %collective-permute-start.22 = (f32[2,4,1,256]{3,2,1,0:T(1,128)S(1)}, f32[2,4,1,256]{3,2,1,0:T(1,128)S(1)}, u32[]{:S(2)}, u32[]{:S(2)}) collective-permute-start(f32[2,4,1,256]{3,2,1,0:T(1,128)S(1)} %get-tuple-element.19), channel_id=1, source_target_pairs={{0,1},{1,2},{2,3},{3,4},{4,5},{5,6},{6,7},{7,0},{8,9},{9,10},{10,1... | collective-permute-start | bytes 24584 | tf_op jit(solution)/shard_map/ppermute | solution.py:17
  83.9 10.6 %collective-permute-start.23 = (f32[2,4,1,256]{3,2,1,0:T(1,128)S(1)}, f32[2,4,1,256]{3,2,1,0:T(1,128)S(1)}, u32[]{:S(2)}, u32[]{:S(2)}) collective-permute-start(f32[2,4,1,256]{3,2,1,0:T(1,128)S(1)} %get-tuple-element.20), channel_id=1, source_target_pairs={{1,0},{2,1},{3,2},{4,3},{5,4},{6,5},{7,6},{0,7},{9,8},{10,9},{11,1... | collective-permute-start | bytes 24584 | tf_op jit(solution)/shard_map/ppermute | solution.py:20
  88.6 7.0 %collective-permute-start.20 = (f32[2,1,128,256]{3,2,1,0:T(8,128)S(1)}, f32[2,1,128,256]{3,2,1,0:T(8,128)S(1)}, u32[]{:S(2)}, u32[]{:S(2)}) collective-permute-start(f32[2,1,128,256]{3,2,1,0:T(8,128)S(1)} %get-tuple-element.17), channel_id=1, source_target_pairs={{0,8},{8,16},{16,24},{1,9},{9,17},{17,25},{2,10},{10,18},{18,26},{... | collective-permute-start | bytes 786440 | tf_op jit(solution)/shard_map/ppermute | solution.py:17
  92.3 7.7 %collective-permute-start.21 = (f32[2,1,128,256]{3,2,1,0:T(8,128)S(1)}, f32[2,1,128,256]{3,2,1,0:T(8,128)S(1)}, u32[]{:S(2)}, u32[]{:S(2)}) collective-permute-start(f32[2,1,128,256]{3,2,1,0:T(8,128)S(1)} %get-tuple-element.18), channel_id=1, source_target_pairs={{8,0},{16,8},{24,16},{9,1},{17,9},{25,17},{10,2},{18,10},{26,18},{... | collective-permute-start | bytes 786440 | tf_op jit(solution)/shard_map/ppermute | solution.py:20
where the time goes:
time: 103 us; the launch traced here: 102 us
  starting transfers between devices  62.2 us (60%)
  other arithmetic  18.3 us (18%)
  waiting for transfers between devices  11 us (11%)
  local copies, waits for them, and re-layouts  9.77 us (9%)
  between operations  1.11 us (1%)
    ppermute x12, starting transfers between devices, with_halo(): lax.ppermute(lax.slice_in_dim(block, 0, width, axis=dim), axis, backward)  37.2 us
    ppermute x12, starting transfers between devices, with_halo(): lax.ppermute(lax.slice_in_dim(block, block.shape[dim] - width, None, axis...  25 us
    ppermute x12, waiting for transfers between devices, with_halo(): lax.ppermute(lax.slice_in_dim(block, 0, width, axis=dim), axis, backward)  6.96 us
    add x3, other arithmetic, voxel_kelvin(): phase_slope(melting_status) * specific_energy_value  6.24 us
    div x3, other arithmetic, mechanics(): (body_force + adjacent_accumulated - correction) / diagonal_total  5.17 us
    ppermute x12, waiting for transfers between devices, with_halo(): lax.ppermute(lax.slice_in_dim(block, block.shape[dim] - width, None, axis...  4.05 us
    mul x2, other arithmetic, mechanics(): correction = modulus * plastic * strain / jnp.maximum(magnitude, 0.1)  3.83 us
    unnamed x21, local copies, waits for them, and re-layouts  2.3 us
  transfers between devices with their start and end apart: 24, of which 7 were waited for; matrix products, arithmetic and copies ran while one was open for 20% of the time, Pallas kernels for 0%

commit v1 on v0

v1 whole, which is shorter than its diff:
```python
import functools
import math

import jax
import jax.numpy as jnp
from jax import lax
from jax.experimental import pallas as pl
from jax.experimental.pallas import tpu as pltpu
from jax.sharding import PartitionSpec as P

HEAT_SWEEPS = 3
SUB = 8
LANE = 128
CHUNKS = 4
PIPES = -2.0
MESH = pl.DeviceIdType.MESH


def weight(t):
    return 0.052 - 0.012 * jnp.tanh(2.0 * t)


def stiffness(t):
    return 2.5 - 1.5 * jnp.tanh(1.5 * t)


def kernel(
    n_ax, n_az, planes, groups,
    h_ref, st_ref, fl_ref, u_ref, h_out, u_out,
    h_raw, st_raw, fl_raw, u_raw, ho_raw, uo_raw,
    T, W, S, H, U, C, row_out, row_in,
    in_sem, out_sem, ax_send, ax_recv, az_send, az_recv,
):
    J = groups
    halves = h_raw.shape[1]
    ax = lax.axis_index("ax")
    az = lax.axis_index("az")
    has_lo = ax > 0
    has_hi = ax < n_ax - 1
    ax_lo, ax_hi = ax - 1, ax + 1
    az_lo = lax.rem(az + n_az - 1, n_az)
    az_hi = lax.rem(az + 1, n_az)

    def whole_in(idx, ref, raw):
        lead = (slice(None),) * (len(ref.shape) - 1)
        return [
            pltpu.make_async_copy(
                ref.at[lead + (pl.ds(q * LANE, LANE),)],
                raw.at[(slice(None),) * (len(ref.shape) - 2) + (q,)],
                in_sem.at[idx, q],
            )
            for q in range(halves)
        ]

    ins = [
        whole_in(i, ref, raw)
        for i, (ref, raw) in enumerate(
            ((h_ref, h_raw), (st_ref, st_raw), (u_ref, u_raw), (fl_ref, fl_raw))
        )
    ]
    for group in ins:
        for copy in group:
            copy.start()

    barrier = pltpu.get_barrier_semaphore()
    pl.semaphore_signal(barrier, inc=1, device_id=(ax, az_lo), device_id_type=MESH)
    pl.semaphore_signal(barrier, inc=1, device_id=(ax, az_hi), device_id_type=MESH)

    @pl.when(has_lo)
    def _():
        pl.semaphore_signal(barrier, inc=1, device_id=(ax_lo, az), device_id_type=MESH)

    @pl.when(has_hi)
    def _():
        pl.semaphore_signal(barrier, inc=1, device_id=(ax_hi, az), device_id_type=MESH)

    def clear(plane):
        def body(j, carry):
            zero = jnp.zeros((SUB, halves * LANE), jnp.float32)
            for k in range(HEAT_SWEEPS + 1):
                T[k, plane, j] = zero
            for m in range(2):
                for c in range(2):
                    U[m, c, plane, j] = zero
            return carry

        lax.fori_loop(1, J + 1, body, 0)

    @pl.when(jnp.logical_not(has_lo))
    def _():
        clear(0)

    @pl.when(jnp.logical_not(has_hi))
    def _():
        clear(planes + 1)

    row_out[...] = jnp.zeros_like(row_out)

    pl.semaphore_wait(barrier, 2 + has_lo.astype(jnp.int32) + has_hi.astype(jnp.int32))

    step = J // CHUNKS
    order = [(c + 1) % CHUNKS for c in range(CHUNKS)]
    NT = HEAT_SWEEPS + 1

    def ax_copy(k, side, c):
        src_plane, dst_plane = (1, planes + 1) if side == 0 else (planes, 0)
        spot = pl.ds(1 + c * step, step)
        if k < NT:
            src, dst = T.at[k, src_plane, spot], T.at[k, dst_plane, spot]
        else:
            src, dst = U.at[k - NT, :, src_plane, spot], U.at[k - NT, :, dst_plane, spot]
        return pltpu.make_async_remote_copy(
            src_ref=src, dst_ref=dst,
            send_sem=ax_send.at[k, side, c], recv_sem=ax_recv.at[k, side, c],
            device_id=(ax_lo if side == 0 else ax_hi, az), device_id_type=MESH,
        )

    def send_ax(k, c):
        @pl.when(has_lo)
        def _():
            ax_copy(k, 0, c).start()

        @pl.when(has_hi)
        def _():
            ax_copy(k, 1, c).start()

    def wait_ax(k, c):
        @pl.when(has_hi)
        def _():
            ax_copy(k, 0, c).wait_recv()

        @pl.when(has_lo)
        def _():
            ax_copy(k, 1, c).wait_recv()

    def az_copy(k, side):
        return pltpu.make_async_remote_copy(
            src_ref=row_out.at[k, side], dst_ref=row_in.at[k, side],
            send_sem=az_send.at[k, side], recv_sem=az_recv.at[k, side],
            device_id=(ax, az_lo if side == 0 else az_hi), device_id_type=MESH,
        )

    def fields(k):
        if k < NT:
            return [(T, (k, p + 1)) for p in range(planes)]
        return [(U, (k - NT, c, p + 1)) for c in range(2) for p in range(planes)]

    def send_az(k, side):
        group, sub = (1, 0) if side == 0 else (J, SUB - 1)
        for i, (ref, at) in enumerate(fields(k)):
            row_out[k, side, i : i + 1, :] = ref[at + (group, pl.ds(sub, 1))]
        az_copy(k, side).start()

    sub_id = lax.broadcasted_iota(jnp.int32, (SUB, halves * LANE), 0)
    lane_id = lax.broadcasted_iota(jnp.int32, (SUB, halves * LANE), 1)
    first_lane = lane_id == 0
    last_lane = lane_id == halves * LANE - 1
    width = halves * LANE

    def wait_az(k, side):
        az_copy(k, side).wait_recv()
        for i, (ref, at) in enumerate(fields(k)):
            row = jnp.broadcast_to(row_in[k, side, i : i + 1, :], (SUB, width))
            if side == 1:
                value = jnp.where(sub_id == 0, row, pltpu.roll(ref[at + (J,)], 1, axis=0))
                spot = at + (0,)
            else:
                value = jnp.where(sub_id == SUB - 1, row, pltpu.roll(ref[at + (1,)], SUB - 1, axis=0))
                spot = at + (J + 1,)
            ref[spot] = value
            if k < NT:
                W[spot] = weight(value) if k < HEAT_SWEEPS else stiffness(value)

    def to_high(x):
        return pltpu.roll(x, width - 1, axis=1)

    def to_low(x):
        return pltpu.roll(x, 1, axis=1)

    def strided(ref, lead, j):
        return jnp.concatenate(
            [ref[lead + (q, pl.ds(j - 1, SUB, stride=J))] for q in range(halves)], axis=1
        )

    def put_strided(ref, lead, j, value):
        for q in range(halves):
            ref[lead + (q, pl.ds(j - 1, SUB, stride=J))] = value[:, q * LANE : (q + 1) * LANE]

    def sends(k, c):
        send_ax(k, c)
        if c == 0:
            send_az(k, 0)
        if c == CHUNKS - 1:
            send_az(k, 1)

    def waits(k, c):
        wait_ax(k, c)
        if c == 0:
            wait_az(k, 1)
        if c == CHUNKS - 1:
            wait_az(k, 0)

    for copy in ins[0] + ins[1]:
        copy.wait()

    def first_temperature(j, carry):
        for p in range(planes):
            h = strided(h_raw, (p,), j)
            st = strided(st_raw, (p,), j)
            s = jnp.where(st == 0, 1.0, jnp.where(st == 1, 0.08, 0.5))
            o = jnp.where(st == 0, -1.0, jnp.where(st == 1, -0.02, 0.0))
            t = s * h + o
            T[0, p + 1, j] = t
            W[0, p + 1, j] = weight(t)
            S[p, j] = s
            H[p, j] = h
        return carry

    for c in order:
        lax.fori_loop(1 + c * step, 1 + (c + 1) * step, first_temperature, 0)
        sends(0, c)

    for copy in ins[2] + ins[3]:
        copy.wait()

    def first_displacement(j, carry):
        for c in range(2):
            for p in range(planes):
                U[0, c, p + 1, j] = strided(u_raw, (c, p), j)
        return carry

    lax.fori_loop(1, J + 1, first_displacement, 0)

    pipe_weight = 0.052 - 0.012 * math.tanh(2.0 * PIPES)

    def heat(k):
        def az_face(p, j):
            return (W[k, p + 1, j] + W[k, p + 1, j + 1]) * (T[k, p + 1, j + 1] - T[k, p + 1, j])

        def body(j, below):
            above = []
            t_lo = T[k, 0, j]
            w_lo = weight(t_lo)
            t, w = T[k, 1, j], W[k, 1, j]
            face = (w + w_lo) * (t - t_lo)
            for p in range(planes):
                if p < planes - 1:
                    t_hi, w_hi = T[k, p + 2, j], W[k, p + 2, j]
                else:
                    t_hi = T[k, planes + 1, j]
                    w_hi = weight(t_hi)
                next_face = (w + w_hi) * (t_hi - t)
                az_high = az_face(p, j)
                net = (next_face - face) + (az_high - below[p])
                radial = (jnp.where(last_lane, pipe_weight, w) + to_high(w)) * (
                    to_high(t) - jnp.where(last_lane, PIPES, t)
                )
                net = net + (jnp.where(last_lane, 0.0, radial) - to_low(radial))
                h = H[p, j] + net
                new = t + S[p, j] * net
                T[k + 1, p + 1, j] = new
                if k < HEAT_SWEEPS - 1:
                    H[p, j] = h
                    W[k + 1, p + 1, j] = weight(new)
                else:
                    put_strided(ho_raw, (p,), j, h)
                    W[k + 1, p + 1, j] = stiffness(new)
                above.append(az_high)
                face, t, w = next_face, t_hi, w_hi
            return tuple(above)

        for c in order:
            waits(k, c)
            start = 1 + c * step
            below = tuple(az_face(p, start - 1) for p in range(planes))
            lax.fori_loop(start, start + step, body, below)
            sends(k + 1, c)
            if k < 2 and c == order[-1]:
                for d in order[2 * k : 2 * k + 2]:
                    sends(NT, d)

    for k in range(HEAT_SWEEPS):
        heat(k)

    def outs(idx, raw, ref):
        lead = (slice(None),) * (len(ref.shape) - 1)
        return [
            pltpu.make_async_copy(
                raw.at[(slice(None),) * (len(ref.shape) - 2) + (q,)],
                ref.at[lead + (pl.ds(q * LANE, LANE),)],
                out_sem.at[idx, q],
            )
            for q in range(halves)
        ]

    h_copies = outs(0, ho_raw, h_out)
    for copy in h_copies:
        copy.start()

    K = HEAT_SWEEPS

    def mechanics(m):
        def az_coef(p, j):
            return W[K, p + 1, j] + W[K, p + 1, j + 1]

        def body(j, below):
            above = []
            e_lo = stiffness(T[K, 0, j])
            e = W[K, 1, j]
            a_lo = e + e_lo
            for p in range(planes):
                e_hi = W[K, p + 2, j] if p < planes - 1 else stiffness(T[K, planes + 1, j])
                a_hi = e + e_hi
                a_up = az_coef(p, j)
                a_down = below[p]
                r_hi = e + jnp.where(last_lane, e, to_high(e))
                r_lo = e + jnp.where(first_lane, e, to_low(e))
                if m == 0:
                    t = T[K, p + 1, j]
                    inverse = 1.0 / (1.0 + ((a_lo + a_hi) + (a_up + a_down) + (r_hi + r_lo)))
                    half = 0.5 * e
                    f0 = half * (
                        jnp.where(last_lane, t, to_high(t)) - jnp.where(first_lane, t, to_low(t))
                    )
                    f1 = half * (T[K, p + 1, j + 1] - T[K, p + 1, j - 1])
                    flags = strided(fl_raw, (p,), j).astype(jnp.float32)
                    rate = flags * 0.6 * jnp.exp(8.0 / 12.0 - 8.0 / (t + 12.0))
                    er = e * rate
                    flow = er / (1.0 + er)
                    C[0, p, j] = inverse
                    C[1, p, j] = f0
                    C[2, p, j] = f1
                    C[3, p, j] = flow
                else:
                    inverse, f0, f1, flow = (C[i, p, j] for i in range(4))
                u0, u1 = U[m, 0, p + 1, j], U[m, 1, p + 1, j]
                u0_hi = jnp.where(last_lane, 0.0, to_high(u0))
                u0_lo = jnp.where(first_lane, 0.0, to_low(u0))
                u1_hi = jnp.where(last_lane, 0.0, to_high(u1))
                u1_lo = jnp.where(first_lane, 0.0, to_low(u1))
                u1_up, u1_down = U[m, 1, p + 1, j + 1], U[m, 1, p + 1, j - 1]
                d0 = u0_hi - u0_lo
                d1 = u1_up - u1_down
                square = 0.25 * (d0 * d0 + d1 * d1)
                root = lax.rsqrt(jnp.maximum(square, 1e-30))
                over = jnp.maximum(e * (square * root) - (0.3 + (e - 1.0) * (1.0 / 6.0)), 0.0)
                factor = flow * over * jnp.minimum(root, 10.0)
                near0 = (
                    (a_lo * U[m, 0, p, j] + a_hi * U[m, 0, p + 2, j])
                    + (a_up * U[m, 0, p + 1, j + 1] + a_down * U[m, 0, p + 1, j - 1])
                    + (r_hi * u0_hi + r_lo * u0_lo)
                )
                near1 = (
                    (a_lo * U[m, 1, p, j] + a_hi * U[m, 1, p + 2, j])
                    + (a_up * u1_up + a_down * u1_down)
                    + (r_hi * u1_hi + r_lo * u1_lo)
                )
                new0 = (f0 + near0 - factor * d0) * inverse
                new1 = (f1 + near1 - factor * d1) * inverse
                if m == 0:
                    U[1, 0, p + 1, j] = new0
                    U[1, 1, p + 1, j] = new1
                else:
                    put_strided(uo_raw, (0, p), j, new0)
                    put_strided(uo_raw, (1, p), j, new1)
                above.append(a_up)
                a_lo, e = a_hi, e_hi
            return tuple(above)

        for c in order:
            if m == 0:
                waits(K, c)
            waits(NT + m, c)
            start = 1 + c * step
            below = tuple(az_coef(p, start - 1) for p in range(planes))
            lax.fori_loop(start, start + step, body, below)
            if m == 0:
                sends(NT + 1, c)

    mechanics(0)
    mechanics(1)

    u_copies = outs(1, uo_raw, u_out)
    for copy in u_copies:
        copy.start()

    for k in range(NT + 2):
        for side in range(2):
            az_copy(k, side).wait_send()

    @pl.when(has_lo)
    def _():
        for k in range(NT + 2):
            for c in range(CHUNKS):
                ax_copy(k, 0, c).wait_send()

    @pl.when(has_hi)
    def _():
        for k in range(NT + 2):
            for c in range(CHUNKS):
                ax_copy(k, 1, c).wait_send()

    for copy in h_copies + u_copies:
        copy.wait()


def on_device(n_ax, n_az, enthalpy, melting_status, plastic_flags, displacement):
    planes, rows, width = enthalpy.shape
    halves = width // LANE
    groups = rows // SUB
    f32 = jnp.float32
    K = HEAT_SWEEPS
    raw = (planes, halves, rows, LANE)
    padded = (planes + 2, groups + 2, SUB, width)
    inner = (planes, groups + 2, SUB, width)
    any_space = pl.BlockSpec(memory_space=pl.ANY)
    exchanges = K + 3
    return pl.pallas_call(
        functools.partial(kernel, n_ax, n_az, planes, groups),
        out_shape=(
            jax.ShapeDtypeStruct(enthalpy.shape, f32),
            jax.ShapeDtypeStruct(displacement.shape, f32),
        ),
        in_specs=[any_space] * 4,
        out_specs=(any_space, any_space),
        scratch_shapes=[
            pltpu.VMEM(raw, f32),
            pltpu.VMEM(raw, jnp.int32),
            pltpu.VMEM(raw, jnp.int32),
            pltpu.VMEM((2,) + raw, f32),
            pltpu.VMEM(raw, f32),
            pltpu.VMEM((2,) + raw, f32),
            pltpu.VMEM((K + 1,) + padded, f32),
            pltpu.VMEM((K + 1,) + padded, f32),
            pltpu.VMEM(inner, f32),
            pltpu.VMEM(inner, f32),
            pltpu.VMEM((2, 2) + padded, f32),
            pltpu.VMEM((4,) + inner, f32),
            pltpu.VMEM((exchanges, 2, 2 * planes, width), f32),
            pltpu.VMEM((exchanges, 2, 2 * planes, width), f32),
            pltpu.SemaphoreType.DMA((4, halves)),
            pltpu.SemaphoreType.DMA((2, halves)),
            pltpu.SemaphoreType.DMA((exchanges, 2, CHUNKS)),
            pltpu.SemaphoreType.DMA((exchanges, 2, CHUNKS)),
            pltpu.SemaphoreType.DMA((exchanges, 2)),
            pltpu.SemaphoreType.DMA((exchanges, 2)),
        ],
        compiler_params=pltpu.CompilerParams(
            collective_id=0, has_side_effects=True, vmem_limit_bytes=40 * 1024 * 1024
        ),
    )(enthalpy, melting_status, plastic_flags, displacement)


def solution(mesh):
    in_specs = (
        P("ax", "az", None),
        P("ax", "az", None),
        P("ax", "az", None),
        P(None, "ax", "az", None),
    )
    out_specs = (P("ax", "az", None), P(None, "ax", "az", None))
    return jax.shard_map(
        functools.partial(on_device, mesh.shape["ax"], mesh.shape["az"]),
        mesh=mesh, in_specs=in_specs, out_specs=out_specs, check_vma=False,
    )
```

time: 103 us -> 38 us (0.37)
  starting transfers between devices: 62.2 us -> 0 us
  Pallas kernels: 0 us -> 31 us
  other arithmetic: 18.3 us -> 0 us
  waiting for transfers between devices: 11 us -> 0 us
  local copies, waits for them, and re-layouts: 9.77 us -> 6.11 us
    ppermute x24 -> x0, starting transfers between devices: 62.2 us -> none  [the longest x12 37.2 us: with_halo(): lax.ppermute(lax.slice_in_dim(block, 0, width, axis=dim), axis, backward)]
    pallas_call x0 -> x1, Pallas kernels: none -> 31 us  [on_device(): pl.pallas_call(functools.partial(kernel, n_ax, n_az, planes, groups), out...]
    ppermute x24 -> x0, waiting for transfers between devices: 11 us -> none  [the longest x12 6.96 us: with_halo(): lax.ppermute(lax.slice_in_dim(block, 0, width, axis=dim), axis, backward)]
    mul x7 -> x0, other arithmetic: 6.48 us -> none  [the longest x2 3.83 us: mechanics(): correction = modulus * plastic * strain / jnp.maximum(magnitude, 0.1)]
    add x3 -> x0, other arithmetic: 6.24 us -> none  [voxel_kelvin(): phase_slope(melting_status) * specific_energy_value]
    div x3 -> x0, other arithmetic: 5.17 us -> none  [mechanics(): (body_force + adjacent_accumulated - correction) / diagonal_total]
    slice x21 -> x0, local copies, waits for them, and re-layouts: 5.13 us -> none  [the longest x10 2.28 us: with_halo(): lax.slice_in_dim(block, block.shape[dim] - width, None, axis=dim)]
    unnamed x21 -> x10, local copies, waits for them, and re-layouts: 2.3 us -> 6.11 us
  transfers between devices with their start and end apart: 24 -> 0, of which waited for: 7 -> 0; matrix products, arithmetic and copies ran while one was open for 20% -> 0% of each run, Pallas kernels for 0% -> 0%
where the time goes in v1:
time: 38 us; the launch traced here: 37.7 us
  Pallas kernels  31 us (82%)
  local copies, waits for them, and re-layouts  6.11 us (16%)
  between operations  0.65 us (2%)
    pallas_call x1, Pallas kernels, on_device(): pl.pallas_call(functools.partial(kernel, n_ax, n_az, planes, groups), out...  31 us
    unnamed x10, local copies, waits for them, and re-layouts  6.11 us

profile of v1, /device:TPU:1, one launch (start us, length us, event | category | flops | bytes accessed | tf_op | source)
XLA Modules:
  0.0 37.7 jit_solution(9698998777554965868)
XLA Ops:
  0.6 0.0 copy-start
  0.6 1.2 %copy-done = f32[2,4,128,256]{3,2,1,0:T(8,128)S(1)} copy-done((f32[2,4,128,256]{3,2,1,0:T(8,128)S(1)}, f32[2,4,128,256]{3,2,1,0:T(8,128)}, u32[]{:S(2)}) %copy-start) | copy-done | bytes 1048600
  1.9 0.0 copy-start.1
  1.9 1.0 %copy-done.1 = f32[4,128,256]{2,1,0:T(8,128)S(1)} copy-done((f32[4,128,256]{2,1,0:T(8,128)S(1)}, f32[4,128,256]{2,1,0:T(8,128)}, u32[]{:S(2)}) %copy-start.1) | copy-done | bytes 524312
  2.9 0.0 copy-start.2
  2.9 1.0 %copy-done.2 = s32[4,128,256]{2,1,0:T(8,128)S(1)} copy-done((s32[4,128,256]{2,1,0:T(8,128)S(1)}, s32[4,128,256]{2,1,0:T(8,128)}, u32[]{:S(2)}) %copy-start.2) | copy-done | bytes 524312
  3.9 0.0 copy-start.3
  3.9 1.0 %copy-done.3 = s32[4,128,256]{2,1,0:T(8,128)S(1)} copy-done((s32[4,128,256]{2,1,0:T(8,128)S(1)}, s32[4,128,256]{2,1,0:T(8,128)}, u32[]{:S(2)}) %copy-start.3) | copy-done | bytes 524312
  5.0 31.0 %shard_map.59 = (f32[4,128,256]{2,1,0:T(8,128)S(1)}, f32[2,4,128,256]{3,2,1,0:T(8,128)S(1)}) custom-call(f32[4,128,256]{2,1,0:T(8,128)S(1)} %copy-done.1, s32[4,128,256]{2,1,0:T(8,128)S(1)} %copy-done.2, s32[4,128,256]{2,1,0:T(8,128)S(1)} %copy-done.3, f32[2,4,128,256]{3,2,1,0:T(8,128)S(1)} %copy-done), custom_call_target="tpu_custom_call" | custom-call | tf_op jit(solution)/shard_map/pallas_call | solution.py:418
  36.0 0.8 %copy.8 = f32[4,128,256]{2,1,0:T(8,128)} copy(f32[4,128,256]{2,1,0:T(8,128)S(1)} %get-tuple-element.4) | data formatting | bytes 1048576
  36.7 1.0 %copy.9 = f32[2,4,128,256]{3,2,1,0:T(8,128)} copy(f32[2,4,128,256]{3,2,1,0:T(8,128)S(1)} %get-tuple-element.5) | data formatting | bytes 2097152
Async XLA Ops:
  0.6 1.2 %copy-start = (f32[2,4,128,256]{3,2,1,0:T(8,128)S(1)}, f32[2,4,128,256]{3,2,1,0:T(8,128)}, u32[]{:S(2)}) copy-start(f32[2,4,128,256]{3,2,1,0:T(8,128)} %u_ref.1) | copy-start | bytes 3145732
  1.9 1.0 %copy-start.1 = (f32[4,128,256]{2,1,0:T(8,128)S(1)}, f32[4,128,256]{2,1,0:T(8,128)}, u32[]{:S(2)}) copy-start(f32[4,128,256]{2,1,0:T(8,128)} %h_ref.1) | copy-start | bytes 1572868
  2.9 1.0 %copy-start.2 = (s32[4,128,256]{2,1,0:T(8,128)S(1)}, s32[4,128,256]{2,1,0:T(8,128)}, u32[]{:S(2)}) copy-start(s32[4,128,256]{2,1,0:T(8,128)} %st_ref.1) | copy-start | bytes 1572868
  3.9 1.0 %copy-start.3 = (s32[4,128,256]{2,1,0:T(8,128)S(1)}, s32[4,128,256]{2,1,0:T(8,128)}, u32[]{:S(2)}) copy-start(s32[4,128,256]{2,1,0:T(8,128)} %fl_ref.1) | copy-start | bytes 1572868

commit v2 on v1

--- a/solution.py
+++ b/solution.py
@@ -11,7 +11,8 @@
 HEAT_SWEEPS = 3
 SUB = 8
 LANE = 128
-CHUNKS = 4
+CHUNKS = 3
+HALO = 8
 PIPES = -2.0
 MESH = pl.DeviceIdType.MESH
 
@@ -28,11 +29,12 @@
     n_ax, n_az, planes, groups,
     h_ref, st_ref, fl_ref, u_ref, h_out, u_out,
     h_raw, st_raw, fl_raw, u_raw, ho_raw, uo_raw,
-    T, W, S, H, U, C, row_out, row_in,
+    T, W, S, H, U, C,
     in_sem, out_sem, ax_send, ax_recv, az_send, az_recv,
 ):
     J = groups
     halves = h_raw.shape[1]
+    rows = h_ref.shape[1]
     ax = lax.axis_index("ax")
     az = lax.axis_index("az")
     has_lo = ax > 0
@@ -46,18 +48,33 @@
         return [
             pltpu.make_async_copy(
                 ref.at[lead + (pl.ds(q * LANE, LANE),)],
-                raw.at[(slice(None),) * (len(ref.shape) - 2) + (q,)],
+                raw.at[(slice(None),) * (len(ref.shape) - 2) + (q, pl.ds(HALO, rows))],
                 in_sem.at[idx, q],
             )
             for q in range(halves)
         ]
 
-    ins = [
-        whole_in(i, ref, raw)
-        for i, (ref, raw) in enumerate(
-            ((h_ref, h_raw), (st_ref, st_raw), (u_ref, u_raw), (fl_ref, fl_raw))
-        )
-    ]
+    pairs = ((h_ref, h_raw), (st_ref, st_raw), (u_ref, u_raw), (fl_ref, fl_raw))
+    ins = [whole_in(i, ref, raw) for i, (ref, raw) in enumerate(pairs)]
+
+    def az_copies(idx, side):
+        ref, raw = pairs[idx]
+        lead = (slice(None),) * (len(ref.shape) - 2)
+        source, target = (0, HALO + rows) if side == 0 else (rows - HALO, 0)
+        return [
+            pltpu.make_async_remote_copy(
+                src_ref=ref.at[lead + (pl.ds(source, HALO), pl.ds(q * LANE, LANE))],
+                dst_ref=raw.at[lead + (q, pl.ds(target, HALO))],
+                send_sem=az_send.at[idx, side, q], recv_sem=az_recv.at[idx, side, q],
+                device_id=(ax, az_lo if side == 0 else az_hi), device_id_type=MESH,
+            )
+            for q in range(halves)
+        ]
+
+    def wait_az(idx):
+        for side in range(2):
+            for copy in az_copies(idx, side):
+                copy.wait_recv()
     for group in ins:
         for copy in group:
             copy.start()
@@ -94,9 +111,11 @@
     def _():
         clear(planes + 1)
 
-    row_out[...] = jnp.zeros_like(row_out)
-
     pl.semaphore_wait(barrier, 2 + has_lo.astype(jnp.int32) + has_hi.astype(jnp.int32))
+    for idx in (0, 1):
+        for side in range(2):
+            for copy in az_copies(idx, side):
+                copy.start()
 
     step = J // CHUNKS
     order = [(c + 1) % CHUNKS for c in range(CHUNKS)]
@@ -133,43 +152,22 @@
         def _():
             ax_copy(k, 1, c).wait_recv()
 
-    def az_copy(k, side):
-        return pltpu.make_async_remote_copy(
-            src_ref=row_out.at[k, side], dst_ref=row_in.at[k, side],
-            send_sem=az_send.at[k, side], recv_sem=az_recv.at[k, side],
-            device_id=(ax, az_lo if side == 0 else az_hi), device_id_type=MESH,
-        )
-
     def fields(k):
         if k < NT:
             return [(T, (k, p + 1)) for p in range(planes)]
         return [(U, (k - NT, c, p + 1)) for c in range(2) for p in range(planes)]
 
-    def send_az(k, side):
-        group, sub = (1, 0) if side == 0 else (J, SUB - 1)
-        for i, (ref, at) in enumerate(fields(k)):
-            row_out[k, side, i : i + 1, :] = ref[at + (group, pl.ds(sub, 1))]
-        az_copy(k, side).start()
-
-    sub_id = lax.broadcasted_iota(jnp.int32, (SUB, halves * LANE), 0)
     lane_id = lax.broadcasted_iota(jnp.int32, (SUB, halves * LANE), 1)
     first_lane = lane_id == 0
     last_lane = lane_id == halves * LANE - 1
     width = halves * LANE
 
-    def wait_az(k, side):
-        az_copy(k, side).wait_recv()
-        for i, (ref, at) in enumerate(fields(k)):
-            row = jnp.broadcast_to(row_in[k, side, i : i + 1, :], (SUB, width))
-            if side == 1:
-                value = jnp.where(sub_id == 0, row, pltpu.roll(ref[at + (J,)], 1, axis=0))
-                spot = at + (0,)
-            else:
-                value = jnp.where(sub_id == SUB - 1, row, pltpu.roll(ref[at + (1,)], SUB - 1, axis=0))
-                spot = at + (J + 1,)
-            ref[spot] = value
-            if k < NT:
-                W[spot] = weight(value) if k < HEAT_SWEEPS else stiffness(value)
+    def pad(k):
+        for ref, at in fields(k):
+            for source, target, turn in ((J, 0, 1), (1, J + 1, SUB - 1)):
+                ref[at + (target,)] = pltpu.roll(ref[at + (source,)], turn, axis=0)
+                if k < NT:
+                    W[at + (target,)] = pltpu.roll(W[at + (source,)], turn, axis=0)
 
     def to_high(x):
         return pltpu.roll(x, width - 1, axis=1)
@@ -186,22 +184,10 @@
         for q in range(halves):
             ref[lead + (q, pl.ds(j - 1, SUB, stride=J))] = value[:, q * LANE : (q + 1) * LANE]
 
-    def sends(k, c):
-        send_ax(k, c)
-        if c == 0:
-            send_az(k, 0)
-        if c == CHUNKS - 1:
-            send_az(k, 1)
-
-    def waits(k, c):
-        wait_ax(k, c)
-        if c == 0:
-            wait_az(k, 1)
-        if c == CHUNKS - 1:
-            wait_az(k, 0)
-
     for copy in ins[0] + ins[1]:
         copy.wait()
+    wait_az(0)
+    wait_az(1)
 
     def first_temperature(j, carry):
         for p in range(planes):
@@ -218,8 +204,13 @@
 
     for c in order:
         lax.fori_loop(1 + c * step, 1 + (c + 1) * step, first_temperature, 0)
-        sends(0, c)
-
+        send_ax(0, c)
+
+    pad(0)
+    for idx in (2, 3):
+        for side in range(2):
+            for copy in az_copies(idx, side):
+                copy.start()
     for copy in ins[2] + ins[3]:
         copy.wait()
 
@@ -228,8 +219,6 @@
             for p in range(planes):
                 U[0, c, p + 1, j] = strided(u_raw, (c, p), j)
         return carry
-
-    lax.fori_loop(1, J + 1, first_displacement, 0)
 
     pipe_weight = 0.052 - 0.012 * math.tanh(2.0 * PIPES)
 
@@ -270,23 +259,28 @@
             return tuple(above)
 
         for c in order:
-            waits(k, c)
+            wait_ax(k, c)
             start = 1 + c * step
             below = tuple(az_face(p, start - 1) for p in range(planes))
-            lax.fori_loop(start, start + step, body, below)
-            sends(k + 1, c)
-            if k < 2 and c == order[-1]:
-                for d in order[2 * k : 2 * k + 2]:
-                    sends(NT, d)
+            lax.fori_loop(start, start + step, body, below, unroll=2)
+            send_ax(k + 1, c)
 
     for k in range(HEAT_SWEEPS):
         heat(k)
+        pad(k + 1)
+        if k == 0:
+            wait_az(2)
+            lax.fori_loop(1, J + 1, first_displacement, 0)
+            pad(NT)
+            for c in order:
+                send_ax(NT, c)
+    wait_az(3)
 
     def outs(idx, raw, ref):
         lead = (slice(None),) * (len(ref.shape) - 1)
         return [
             pltpu.make_async_copy(
-                raw.at[(slice(None),) * (len(ref.shape) - 2) + (q,)],
+                raw.at[(slice(None),) * (len(ref.shape) - 2) + (q, pl.ds(HALO, rows))],
                 ref.at[lead + (pl.ds(q * LANE, LANE),)],
                 out_sem.at[idx, q],
             )
@@ -369,24 +363,26 @@
 
         for c in order:
             if m == 0:
-                waits(K, c)
-            waits(NT + m, c)
+                wait_ax(K, c)
+            wait_ax(NT + m, c)
             start = 1 + c * step
             below = tuple(az_coef(p, start - 1) for p in range(planes))
-            lax.fori_loop(start, start + step, body, below)
+            lax.fori_loop(start, start + step, body, below, unroll=2)
             if m == 0:
-                sends(NT + 1, c)
+                send_ax(NT + 1, c)
 
     mechanics(0)
+    pad(NT + 1)
     mechanics(1)
 
     u_copies = outs(1, uo_raw, u_out)
     for copy in u_copies:
         copy.start()
 
-    for k in range(NT + 2):
+    for idx in range(4):
         for side in range(2):
-            az_copy(k, side).wait_send()
+            for copy in az_copies(idx, side):
+                copy.wait_send()
 
     @pl.when(has_lo)
     def _():
@@ -407,10 +403,10 @@
 def on_device(n_ax, n_az, enthalpy, melting_status, plastic_flags, displacement):
     planes, rows, width = enthalpy.shape
     halves = width // LANE
-    groups = rows // SUB
+    groups = (rows + 2 * HALO) // SUB
     f32 = jnp.float32
     K = HEAT_SWEEPS
-    raw = (planes, halves, rows, LANE)
+    raw = (planes, halves, rows + 2 * HALO, LANE)
     padded = (planes + 2, groups + 2, SUB, width)
     inner = (planes, groups + 2, SUB, width)
     any_space = pl.BlockSpec(memory_space=pl.ANY)
@@ -436,17 +432,15 @@
             pltpu.VMEM(inner, f32),
             pltpu.VMEM((2, 2) + padded, f32),
             pltpu.VMEM((4,) + inner, f32),
-            pltpu.VMEM((exchanges, 2, 2 * planes, width), f32),
-            pltpu.VMEM((exchanges, 2, 2 * planes, width), f32),
             pltpu.SemaphoreType.DMA((4, halves)),
             pltpu.SemaphoreType.DMA((2, halves)),
             pltpu.SemaphoreType.DMA((exchanges, 2, CHUNKS)),
             pltpu.SemaphoreType.DMA((exchanges, 2, CHUNKS)),
-            pltpu.SemaphoreType.DMA((exchanges, 2)),
-            pltpu.SemaphoreType.DMA((exchanges, 2)),
+            pltpu.SemaphoreType.DMA((4, 2, halves)),
+            pltpu.SemaphoreType.DMA((4, 2, halves)),
         ],
         compiler_params=pltpu.CompilerParams(
-            collective_id=0, has_side_effects=True, vmem_limit_bytes=40 * 1024 * 1024
+            collective_id=0, has_side_effects=True, vmem_limit_bytes=60 * 1024 * 1024
         ),
     )(enthalpy, melting_status, plastic_flags, displacement)
 

time: 38 us -> 38.2 us (level)
  Pallas kernels: 31 us -> 34.5 us
  local copies, waits for them, and re-layouts: 6.11 us -> 2.93 us
    pallas_call x1, Pallas kernels: 31 us -> 34.5 us  [on_device(): pl.pallas_call(functools.partial(kernel, n_ax, n_az, planes, groups), out...]
    unnamed x10 -> x4, local copies, waits for them, and re-layouts: 6.11 us -> 2.93 us
where the time goes in v2:
time: 38.2 us; the launch traced here: 38.1 us
  Pallas kernels  34.5 us (90%)
  local copies, waits for them, and re-layouts  2.93 us (8%)
  between operations  0.65 us (2%)
    pallas_call x1, Pallas kernels, on_device(): pl.pallas_call(functools.partial(kernel, n_ax, n_az, planes, groups), out...  34.5 us
    unnamed x4, local copies, waits for them, and re-layouts  2.93 us

profile of v2, /device:TPU:1, one launch (start us, length us, event | category | flops | bytes accessed | tf_op | source)
XLA Modules:
  0.0 38.1 jit_solution(2437120125690573122)
XLA Ops:
  0.6 34.5 %shard_map.59 = (f32[4,128,256]{2,1,0:T(8,128)}, f32[2,4,128,256]{3,2,1,0:T(8,128)}) custom-call(f32[4,128,256]{2,1,0:T(8,128)} %h_ref.1, s32[4,128,256]{2,1,0:T(8,128)} %st_ref.1, s32[4,128,256]{2,1,0:T(8,128)} %fl_ref.1, f32[2,4,128,256]{3,2,1,0:T(8,128)} %u_ref.1), custom_call_target="tpu_custom_call" | custom-call | tf_op jit(solution)/shard_map/pallas_call | solution.py:414
  35.1 0.0 copy-start
  35.1 2.0 %copy.8 = f32[4,128,256]{2,1,0:T(8,128)} copy(f32[4,128,256]{2,1,0:T(8,128)} %get-tuple-element.4) | data formatting | bytes 1048576
  37.1 0.0 copy-done
  37.1 1.0 %copy.9 = f32[2,4,128,256]{3,2,1,0:T(8,128)} copy(f32[2,4,128,256]{3,2,1,0:T(8,128)S(1)} %copy-done) | data formatting | bytes 2097152
Async XLA Ops:
  35.1 2.0 %copy-start = (f32[2,4,128,256]{3,2,1,0:T(8,128)S(1)}, f32[2,4,128,256]{3,2,1,0:T(8,128)}, u32[]{:S(2)}) copy-start(f32[2,4,128,256]{3,2,1,0:T(8,128)} %get-tuple-element.5) | copy-start | bytes 3145732

commit v3 on v2

--- a/solution.py
+++ b/solution.py
@@ -9,10 +9,12 @@
 from jax.sharding import PartitionSpec as P
 
 HEAT_SWEEPS = 3
+MECH_SWEEPS = 2
 SUB = 8
 LANE = 128
 CHUNKS = 3
 HALO = 8
+REACH = (HEAT_SWEEPS + MECH_SWEEPS, HEAT_SWEEPS + MECH_SWEEPS, MECH_SWEEPS, MECH_SWEEPS - 1)
 PIPES = -2.0
 MESH = pl.DeviceIdType.MESH
 
@@ -60,11 +62,12 @@
     def az_copies(idx, side):
         ref, raw = pairs[idx]
         lead = (slice(None),) * (len(ref.shape) - 2)
-        source, target = (0, HALO + rows) if side == 0 else (rows - HALO, 0)
+        reach = REACH[idx]
+        source, target = (0, HALO + rows) if side == 0 else (rows - reach, HALO - reach)
         return [
             pltpu.make_async_remote_copy(
-                src_ref=ref.at[lead + (pl.ds(source, HALO), pl.ds(q * LANE, LANE))],
-                dst_ref=raw.at[lead + (q, pl.ds(target, HALO))],
+                src_ref=ref.at[lead + (pl.ds(source, reach), pl.ds(q * LANE, LANE))],
+                dst_ref=raw.at[lead + (q, pl.ds(target, reach))],
                 send_sem=az_send.at[idx, side, q], recv_sem=az_recv.at[idx, side, q],
                 device_id=(ax, az_lo if side == 0 else az_hi), device_id_type=MESH,
             )
@@ -78,6 +81,14 @@
     for group in ins:
         for copy in group:
             copy.start()
+
+    for ref, raw in pairs:
+        for lead in ((c, p) for c in range(2) for p in range(planes)) if len(raw.shape) == 5 else (
+            (p,) for p in range(planes)
+        ):
+            for q in range(halves):
+                for start in (0, HALO + rows):
+                    raw[lead + (q, pl.ds(start, HALO))] = jnp.zeros((HALO, LANE), raw.dtype)
 
     barrier = pltpu.get_barrier_semaphore()
     pl.semaphore_signal(barrier, inc=1, device_id=(ax, az_lo), device_id_type=MESH)
@@ -112,7 +123,7 @@
         clear(planes + 1)
 
     pl.semaphore_wait(barrier, 2 + has_lo.astype(jnp.int32) + has_hi.astype(jnp.int32))
-    for idx in (0, 1):
+    for idx in range(4):
         for side in range(2):
             for copy in az_copies(idx, side):
                 copy.start()
@@ -207,12 +218,9 @@
         send_ax(0, c)
 
     pad(0)
-    for idx in (2, 3):
-        for side in range(2):
-            for copy in az_copies(idx, side):
-                copy.start()
     for copy in ins[2] + ins[3]:
         copy.wait()
+    wait_az(2)
 
     def first_displacement(j, carry):
         for c in range(2):
@@ -262,18 +270,17 @@
             wait_ax(k, c)
             start = 1 + c * step
             below = tuple(az_face(p, start - 1) for p in range(planes))
-            lax.fori_loop(start, start + step, body, below, unroll=2)
+            lax.fori_loop(start, start + step, body, below, unroll=3)
             send_ax(k + 1, c)
 
+    lax.fori_loop(1, J + 1, first_displacement, 0)
+    pad(NT)
+    send_ax(NT, order[0])
     for k in range(HEAT_SWEEPS):
         heat(k)
         pad(k + 1)
-        if k == 0:
-            wait_az(2)
-            lax.fori_loop(1, J + 1, first_displacement, 0)
-            pad(NT)
-            for c in order:
-                send_ax(NT, c)
+        if k < HEAT_SWEEPS - 1:
+            send_ax(NT, order[k + 1])
     wait_az(3)
 
     def outs(idx, raw, ref):
@@ -281,7 +288,7 @@
         return [
             pltpu.make_async_copy(
                 raw.at[(slice(None),) * (len(ref.shape) - 2) + (q, pl.ds(HALO, rows))],
-                ref.at[lead + (pl.ds(q * LANE, LANE),)],
+                ref.at[(slice(None),) * (len(ref.shape) - 2) + (slice(None), pl.ds(q * LANE, LANE))],
                 out_sem.at[idx, q],
             )
             for q in range(halves)
@@ -367,7 +374,7 @@
             wait_ax(NT + m, c)
             start = 1 + c * step
             below = tuple(az_coef(p, start - 1) for p in range(planes))
-            lax.fori_loop(start, start + step, body, below, unroll=2)
+            lax.fori_loop(start, start + step, body, below, unroll=3)
             if m == 0:
                 send_ax(NT + 1, c)
 
@@ -398,6 +405,27 @@
 
     for copy in h_copies + u_copies:
         copy.wait()
+
+
+def hand_on(h_in, u_in, h_out, u_out, h_held, u_held, in_sem, out_sem):
+    planes = h_in.shape[0]
+    parts = [(h_in, h_held, h_out, (p,)) for p in range(planes)]
+    parts += [(u_in, u_held, u_out, (c, p)) for c in range(2) for p in range(planes)]
+    fetches = [
+        pltpu.make_async_copy(source.at[at], held.at[at], in_sem.at[i])
+        for i, (source, held, target, at) in enumerate(parts)
+    ]
+    writes = [
+        pltpu.make_async_copy(held.at[at], target.at[at], out_sem.at[i])
+        for i, (source, held, target, at) in enumerate(parts)
+    ]
+    for fetch in fetches:
+        fetch.start()
+    for fetch, write in zip(fetches, writes):
+        fetch.wait()
+        write.start()
+    for write in writes:
+        write.wait()
 
 
 def on_device(n_ax, n_az, enthalpy, melting_status, plastic_flags, displacement):
@@ -411,12 +439,13 @@
     inner = (planes, groups + 2, SUB, width)
     any_space = pl.BlockSpec(memory_space=pl.ANY)
     exchanges = K + 3
-    return pl.pallas_call(
+    out_shape = (
+        jax.ShapeDtypeStruct(enthalpy.shape, f32),
+        jax.ShapeDtypeStruct(displacement.shape, f32),
+    )
+    results = pl.pallas_call(
         functools.partial(kernel, n_ax, n_az, planes, groups),
-        out_shape=(
-            jax.ShapeDtypeStruct(enthalpy.shape, f32),
-            jax.ShapeDtypeStruct(displacement.shape, f32),
-        ),
+        out_shape=out_shape,
         in_specs=[any_space] * 4,
         out_specs=(any_space, any_space),
         scratch_shapes=[
@@ -443,6 +472,18 @@
             collective_id=0, has_side_effects=True, vmem_limit_bytes=60 * 1024 * 1024
         ),
     )(enthalpy, melting_status, plastic_flags, displacement)
+    return pl.pallas_call(
+        hand_on,
+        out_shape=out_shape,
+        in_specs=[any_space] * 2,
+        out_specs=(any_space, any_space),
+        scratch_shapes=[
+            pltpu.VMEM(enthalpy.shape, f32),
+            pltpu.VMEM(displacement.shape, f32),
+            pltpu.SemaphoreType.DMA((3 * planes,)),
+            pltpu.SemaphoreType.DMA((3 * planes,)),
+        ],
+    )(*results)
 
 
 def solution(mesh):

time: 38.2 us -> 32.8 us (0.86)
  local copies, waits for them, and re-layouts: 2.93 us -> 0 us
  Pallas kernels: 34.5 us -> 32 us
    pallas_call x1, Pallas kernels: 34.5 us -> 29.7 us  [on_device(): pl.pallas_call(functools.partial(kernel, n_ax, n_az, planes, groups), out...]
    unnamed x4 -> x0, local copies, waits for them, and re-layouts: 2.93 us -> none
    pallas_call x0 -> x1, Pallas kernels: none -> 2.33 us  [on_device(): pl.pallas_call(hand_on, out_shape=out_shape, in_specs=[any_space] * 2, ou...]
where the time goes in v3:
time: 32.8 us; the launch traced here: 32.7 us
  Pallas kernels  32 us (98%)
  between operations  0.64 us (2%)
    pallas_call x1, Pallas kernels, on_device(): pl.pallas_call(functools.partial(kernel, n_ax, n_az, planes, groups), out...  29.7 us
    pallas_call x1, Pallas kernels, on_device(): pl.pallas_call(hand_on, out_shape=out_shape, in_specs=[any_space] * 2, ou...  2.33 us

profile of v3, /device:TPU:1, one launch (start us, length us, event | category | flops | bytes accessed | tf_op | source)
XLA Modules:
  0.0 32.7 jit_solution(3687038565906129383)
XLA Ops:
  0.6 29.7 %shard_map.59 = (f32[4,128,256]{2,1,0:T(8,128)}, f32[2,4,128,256]{3,2,1,0:T(8,128)}) custom-call(f32[4,128,256]{2,1,0:T(8,128)} %h_ref.1, s32[4,128,256]{2,1,0:T(8,128)} %st_ref.1, s32[4,128,256]{2,1,0:T(8,128)} %fl_ref.1, f32[2,4,128,256]{3,2,1,0:T(8,128)} %u_ref.1), custom_call_target="tpu_custom_call" | custom-call | tf_op jit(solution)/shard_map/pallas_call | solution.py:446
  30.4 2.3 %shard_map.60 = (f32[4,128,256]{2,1,0:T(8,128)}, f32[2,4,128,256]{3,2,1,0:T(8,128)}) custom-call(f32[4,128,256]{2,1,0:T(8,128)} %get-tuple-element.4.h_in, f32[2,4,128,256]{3,2,1,0:T(8,128)} %get-tuple-element.5.u_in), custom_call_target="tpu_custom_call" | custom-call | tf_op jit(solution)/shard_map/pallas_call | solution.py:475
